TPU v7x, 512 devices: a whole 4x8x8 slice. The times are simulated.
512 devices in a mesh: section: 8 (over y), expert: 64 (over x, z, core).
Axes of the slice: x: 4, y: 8, z: 8, core: 2. Of those that a mesh axis runs over, the one named last changes fastest.
Arguments:
- layer_input: bfloat16 [8, 4096, 2048], P('section', 'expert'), may hold values from -6 to 6
- out_grad: bfloat16 [8, 4096, 2048], P('section', 'expert'), may hold values from -6 to 6
- norm_gain: float32 [8, 2048], P('section'), may hold values from 0.5 to 1.5
- expert_ids: int32 [8, 4096, 8], P('section', 'expert'), may hold values from 0 to 127, all different within a row; in each aligned block of 64 rows (0 to 63, 64 to 127, ..., all dimensions but the last counted through in order) at most 8 rows name the same one
- combine: bfloat16 [8, 4096, 8], P('section', 'expert'), may hold values from 0.049804688 to 0.29882812
- w_gate: bfloat16 [8, 12288, 2048], P('section', 'expert'), may hold values from -0.125 to 0.125
- w_up: bfloat16 [8, 12288, 2048], P('section', 'expert'), may hold values from -0.125 to 0.125
- w_down: bfloat16 [8, 12288, 2048], P('section', 'expert'), may hold values from -0.21875 to 0.21875
Outputs:
- passed_grad: bfloat16 [8, 4096, 2048], P('section', 'expert')
- comb_grad: bfloat16 [8, 4096, 8], P('section', 'expert')
- gain_grad: float32 [8, 2048], P('section')
Inputs may be any that keep to these rules, and one draw needn't show every extreme that they name: `expert_ids`: A token names 8 different experts. Within the tokens of one device (aligned blocks of 64 tokens of a section) no expert is named by more than 8 tokens, a bound that some block reaches.
All inputs are finite; a program needn't handle non-finite values.
Results may differ from a plain program's by a relative error of at most 0.0075.
Values may be sent and summed in bfloat16 or wider, within the bound.
A program may use at most 64 MiB of HBM per device.

v0:
```python
import jax
import jax.numpy as jnp
from jax import lax
from jax.sharding import PartitionSpec as P

EXPERTS = 16
CAP = 8
epsilon = 1e-06


def from_behind(block, axis, distance):
    devices = range(lax.axis_size(axis))
    route = [(i - distance, i) for i in devices if i - distance in devices]
    return lax.ppermute(block, axis, route)


def contract_cols(left, right):
    return lax.dot_general(
        left, right, (((1,), (1,)), ((), ())), preferred_element_type=jnp.float32
    )


def exact_rows(left, right):
    return lax.dot_general(
        left,
        right,
        (((0,), (0,)), ((), ())),
        preferred_element_type=jnp.float32,
        precision=lax.Precision.HIGHEST,
    )


def forward_part(rows_x, weight_gate, weight_up, weight_down):
    gate = contract_cols(rows_x, weight_gate)
    upper = contract_cols(rows_x, weight_up)
    sigma = jax.nn.sigmoid(gate)
    active = gate * sigma
    hidden = (active * upper).astype(jnp.bfloat16)
    output = jnp.dot(hidden, weight_down, preferred_element_type=jnp.float32)
    return (gate, upper, sigma, active, hidden, output)


def backward_part(rows_dy, rows_w, early, weight_gate, weight_up, weight_down):
    gate, upper, sigma, active, hidden, output = early
    comb_part = jnp.sum(rows_dy.astype(jnp.float32) * output, axis=-1).astype(jnp.bfloat16)
    scaled = (rows_w.astype(jnp.float32)[:, None] * rows_dy.astype(jnp.float32)).astype(
        jnp.bfloat16
    )
    hidden_grad = contract_cols(scaled, weight_down)
    gate_part = (hidden_grad * upper * sigma * (1.0 + gate * (1.0 - sigma))).astype(jnp.bfloat16)
    up_part = (hidden_grad * active).astype(jnp.bfloat16)
    rows_grad = (
        jnp.dot(gate_part, weight_gate, preferred_element_type=jnp.float32)
        + jnp.dot(up_part, weight_up, preferred_element_type=jnp.float32)
    ).astype(jnp.bfloat16)
    return (rows_grad, comb_part)


def per_device(layer_input, out_grad, norm_gain, expert_ids, combine, w_gate, w_up, w_down):
    inputs = layer_input[0]
    incoming_gradient = out_grad[0]
    scale_factors = norm_gain[0]
    choices = expert_ids[0]
    weights = combine[0]
    weight_gate = w_gate[0]
    weight_up = w_up[0]
    weight_down = w_down[0]
    tokens_here, width = inputs.shape
    top_count = choices.shape[1]
    peers = lax.axis_size("expert")
    sharing = peers // EXPERTS
    route_count = tokens_here * top_count
    slot_total = EXPERTS * CAP
    peer_slots = peers * CAP
    float_values = inputs.astype(jnp.float32)
    reciprocal_norm = lax.rsqrt(
        jnp.mean(float_values * float_values, axis=-1, keepdims=True) + epsilon
    )
    normalized_rows = float_values * reciprocal_norm
    normalized_input = (normalized_rows * scale_factors[None, :]).astype(jnp.bfloat16)
    flat_ids = choices.reshape(route_count)
    onehot = (flat_ids[:, None] == jnp.arange(EXPERTS, dtype=jnp.int32)[None, :]).astype(jnp.int32)
    before = jnp.cumsum(onehot, axis=0) - onehot
    slot = jnp.sum(before * onehot, axis=1)
    target = flat_ids * CAP + slot
    route_pick = (target[None, :] == jnp.arange(slot_total, dtype=jnp.int32)[:, None]).astype(
        jnp.bfloat16
    )
    token_pick = jnp.sum(route_pick.reshape(slot_total, tokens_here, top_count), axis=-1)
    send_x = jnp.dot(token_pick, normalized_input, preferred_element_type=jnp.float32).astype(
        jnp.bfloat16
    )
    send_x = jnp.repeat(send_x.reshape(EXPERTS, CAP, width), sharing, axis=0)
    send_dy = jnp.dot(token_pick, incoming_gradient, preferred_element_type=jnp.float32).astype(
        jnp.bfloat16
    )
    send_dy = jnp.repeat(send_dy.reshape(EXPERTS, CAP, width), sharing, axis=0)
    send_w = jnp.dot(
        route_pick, weights.reshape(route_count, 1), preferred_element_type=jnp.float32
    )
    send_w = jnp.repeat(send_w.astype(jnp.bfloat16).reshape(EXPERTS, CAP), sharing, axis=0)
    early = None
    rows_x, rows_dy, rows_w = (
        lax.all_to_all(send_x, "expert", split_axis=0, concat_axis=0, tiled=True),
        lax.all_to_all(send_dy, "expert", split_axis=0, concat_axis=0, tiled=True),
        lax.all_to_all(send_w, "expert", split_axis=0, concat_axis=0, tiled=True),
    )
    flat_rows = rows_x.reshape(peer_slots, width)
    early = forward_part(flat_rows, weight_gate, weight_up, weight_down)
    rows_grad, comb_part = backward_part(
        rows_dy.reshape(peer_slots, width),
        rows_w.reshape(peer_slots),
        early,
        weight_gate,
        weight_up,
        weight_down,
    )
    back_rows, back_comb = (
        lax.all_to_all(
            rows_grad.reshape(peers, CAP, width), "expert", split_axis=0, concat_axis=0, tiled=True
        ),
        lax.all_to_all(
            comb_part.reshape(peers, CAP), "expert", split_axis=0, concat_axis=0, tiled=True
        ),
    )
    summed_rows = jnp.sum(
        back_rows.reshape(EXPERTS, sharing, CAP, width).astype(jnp.float32), axis=1
    )
    summed_comb = jnp.sum(back_comb.reshape(EXPERTS, sharing, CAP).astype(jnp.float32), axis=1)
    normalized_gradient = exact_rows(
        token_pick.astype(jnp.float32), summed_rows.reshape(slot_total, width)
    )
    comb_out = exact_rows(route_pick.astype(jnp.float32), summed_comb.reshape(slot_total, 1))
    comb_out = comb_out.astype(jnp.bfloat16).reshape(tokens_here, top_count)
    gain_correction = jnp.sum(normalized_gradient * normalized_rows, axis=0)
    scaled_gradient = normalized_gradient * scale_factors[None, :]
    inner_product = jnp.mean(scaled_gradient * normalized_rows, axis=-1, keepdims=True)
    input_gradient = (
        incoming_gradient.astype(jnp.float32)
        + reciprocal_norm * (scaled_gradient - normalized_rows * inner_product)
    ).astype(jnp.bfloat16)
    passed = from_behind(input_gradient, "section", -1)
    gain_total = lax.psum(gain_correction, "expert")
    return (passed[None], comb_out[None], gain_total[None])


def solution(mesh):
    placed = (
        P("section", "expert", None),
        P("section", "expert", None),
        P("section", None),
        P("section", "expert", None),
        P("section", "expert", None),
        P("section", "expert", None),
        P("section", "expert", None),
        P("section", "expert", None),
    )
    return jax.shard_map(
        per_device,
        mesh=mesh,
        in_specs=placed,
        out_specs=(P("section", "expert", None), P("section", "expert", None), P("section", None)),
        check_vma=False,
    )
```

profile of v0, /device:TPU:56, one launch (start us, length us, event | category | flops | bytes accessed | tf_op | source)
XLA Modules:
  0.0 356.8 jit_solution(8759035831997450475)
XLA Ops:
  0.6 0.8 copy.33
  1.7 0.8 copy.37
  2.6 1.2 reduce-window.6
  4.4 0.6 copy.38
  5.0 13.8 %all-to-all-start = ((bf16[64,1,8]{2,1,0:T(2,128)(2,1)}), bf16[64,1,8]{2,1,0:T(2,128)(2,1)S(1)}, u32[]{:S(2)}, u32[]{:S(2)}) async-start(bf16[64,1,8]{2,1,0:T(2,128)(2,1)} %copy.38), calls=%async_computation | async-start | bytes 65536 | tf_op jit(solution)/shard_map/all_to_all | solution.py:106
  18.9 1.1 fusion.35
  20.2 1.3 fusion.5
  21.5 6.7 %all-to-all-done = bf16[64,1,8]{2,1,0:T(2,128)(2,1)S(1)} async-done(((bf16[64,1,8]{2,1,0:T(2,128)(2,1)}), bf16[64,1,8]{2,1,0:T(2,128)(2,1)S(1)}, u32[]{:S(2)}, u32[]{:S(2)}) %all-to-all-start) | async-done | bytes 1056 | tf_op jit(solution)/shard_map/all_to_all | solution.py:106
  28.2 1.6 broadcast_in_dim.23
  29.9 4.7 %all-to-all-start.2 = ((bf16[64,8,2048]{2,1,0:T(8,128)(2,1)}), bf16[64,8,2048]{2,1,0:T(8,128)(2,1)S(1)}, u32[]{:S(2)}, u32[]{:S(2)}) async-start(bf16[64,8,2048]{2,1,0:T(8,128)(2,1)} %bitcast.14), calls=%async_computation.2 | async-start | bytes 4194304 | tf_op jit(solution)/shard_map/all_to_all | solution.py:104
  34.6 1.3 fusion.4
  35.8 49.9 %all-to-all-done.2 = bf16[64,8,2048]{2,1,0:T(8,128)(2,1)S(1)} async-done(((bf16[64,8,2048]{2,1,0:T(8,128)(2,1)}), bf16[64,8,2048]{2,1,0:T(8,128)(2,1)S(1)}, u32[]{:S(2)}, u32[]{:S(2)}) %all-to-all-start.2) | async-done | bytes 2097184 | tf_op jit(solution)/shard_map/all_to_all | solution.py:104
  85.7 1.8 broadcast_in_dim.22
  87.7 5.9 %all-to-all-start.1 = ((bf16[64,8,2048]{2,1,0:T(8,128)(2,1)}), bf16[64,8,2048]{2,1,0:T(8,128)(2,1)S(1)}, u32[]{:S(2)}, u32[]{:S(2)}) async-start(bf16[64,8,2048]{2,1,0:T(8,128)(2,1)} %bitcast.8), calls=%async_computation.1 | async-start | bytes 4194304 | tf_op jit(solution)/shard_map/all_to_all | solution.py:105
  93.7 2.6 fusion.9
  96.3 1.6 fusion.11
  97.9 46.9 %all-to-all-done.1 = bf16[64,8,2048]{2,1,0:T(8,128)(2,1)S(1)} async-done(((bf16[64,8,2048]{2,1,0:T(8,128)(2,1)}), bf16[64,8,2048]{2,1,0:T(8,128)(2,1)S(1)}, u32[]{:S(2)}, u32[]{:S(2)}) %all-to-all-start.1) | async-done | bytes 2097184 | tf_op jit(solution)/shard_map/all_to_all | solution.py:105
  144.8 2.1 fusion.7
  146.9 0.8 fusion.17
  147.8 0.3 copy-done.6
  148.1 0.8 fusion.3
  148.8 56.9 %all_to_all.30 = bf16[64,8,2048]{2,1,0:T(8,128)(2,1)S(1)} all-to-all(bf16[64,8,2048]{2,1,0:T(8,128)(2,1)S(1)} %fusion.3), channel_id=1, replica_groups=mesh['section'=8,'expert'=64] {'expert'}, dimensions={0} | all-to-all | bytes 4194304 | tf_op jit(solution)/shard_map/all_to_all | solution.py:119
  205.7 0.4 convert_reduce_fusion
  206.1 0.6 copy-done.1
  206.7 0.7 fusion.34
  207.4 0.9 fusion.33
  208.3 3.3 collective-permute-start
  211.6 0.9 fusion.2
  212.6 15.2 %all_to_all.31 = bf16[64,1,8]{2,1,0:T(2,128)(2,1)S(1)} all-to-all(bf16[64,1,8]{2,1,0:T(2,128)(2,1)S(1)} %convert_element_type.145), channel_id=1, replica_groups=mesh['section'=8,'expert'=64] {'expert'}, dimensions={0} | all-to-all | bytes 2048 | tf_op jit(solution)/shard_map/all_to_all | solution.py:122
  228.2 0.7 copy.40
  228.9 127.2 %psum.7 = f32[1,2048]{1,0:T(1,128)} all-reduce(f32[1,2048]{1,0:T(1,128)S(1)} %bitcast.102), channel_id=1, replica_groups=mesh['section'=8,'expert'=64] {'expert'}, use_global_device_ids=true, to_apply=%region_10.11 | all-reduce | flops 2048 | bytes 16384 | tf_op jit(solution)/shard_map/psum | solution.py:143
  356.1 0.7 copy.44
  (44 shorter events, 2.0 us)
Async XLA Ops:
  0.6 93.0 %copy-start = (bf16[1,192,2048]{2,1,0:T(8,128)(2,1)S(1)}, bf16[1,192,2048]{2,1,0:T(8,128)(2,1)}, u32[]{:S(2)}) copy-start(bf16[1,192,2048]{2,1,0:T(8,128)(2,1)} %param.13) | copy-start | bytes 2359300
  5.0 23.2 %all-to-all-start = ((bf16[64,1,8]{2,1,0:T(2,128)(2,1)}), bf16[64,1,8]{2,1,0:T(2,128)(2,1)S(1)}, u32[]{:S(2)}, u32[]{:S(2)}) async-start(bf16[64,1,8]{2,1,0:T(2,128)(2,1)} %copy.38), calls=%async_computation | async-start | bytes 65536 | tf_op jit(solution)/shard_map/all_to_all | solution.py:106
  29.9 55.9 %all-to-all-start.2 = ((bf16[64,8,2048]{2,1,0:T(8,128)(2,1)}), bf16[64,8,2048]{2,1,0:T(8,128)(2,1)S(1)}, u32[]{:S(2)}, u32[]{:S(2)}) async-start(bf16[64,8,2048]{2,1,0:T(8,128)(2,1)} %bitcast.14), calls=%async_computation.2 | async-start | bytes 4194304 | tf_op jit(solution)/shard_map/all_to_all | solution.py:104
  85.7 2.0 copy-start.2
  87.7 57.1 %all-to-all-start.1 = ((bf16[64,8,2048]{2,1,0:T(8,128)(2,1)}), bf16[64,8,2048]{2,1,0:T(8,128)(2,1)S(1)}, u32[]{:S(2)}, u32[]{:S(2)}) async-start(bf16[64,8,2048]{2,1,0:T(8,128)(2,1)} %bitcast.8), calls=%async_computation.1 | async-start | bytes 4194304 | tf_op jit(solution)/shard_map/all_to_all | solution.py:105
  93.7 2.6 copy-start.3
  93.7 2.6 copy-start.5
  144.8 2.1 copy-start.7
  146.9 1.1 copy-start.6
  205.7 1.0 copy-start.1
  205.7 1.0 copy-start.8
  205.7 1.7 copy-start.4
  206.6 4.9 %copy-start.9 = (bf16[1,192,2048]{2,1,0:T(8,128)(2,1)S(1)}, bf16[1,192,2048]{2,1,0:T(8,128)(2,1)}, u32[]{:S(2)}) copy-start(bf16[1,192,2048]{2,1,0:T(8,128)(2,1)} %param.15) | copy-start | bytes 2359300
  208.3 147.8 %collective-permute-start = (bf16[64,2048]{1,0:T(8,128)(2,1)}, bf16[64,2048]{1,0:T(8,128)(2,1)S(1)}, u32[]{:S(2)}, u32[]{:S(2)}) collective-permute-start(bf16[64,2048]{1,0:T(8,128)(2,1)} %fusion.33), channel_id=1, source_target_pairs={{64,0},{128,64},{192,128},{256,192},{320,256},{384,320},{448,384},... | collective-permute-start | bytes 786440 | tf_op jit(solution)/shard_map/ppermute | solution.py:14
where the time goes:
time: 357 us
  blocking collectives  199 us (56%)
  waiting for transfers between devices  104 us (29%)
  starting transfers between devices  27.6 us (8%)
  matrix products  12.4 us (3%)
  local copies, waits for them, and re-layouts  9.12 us (3%)
  other arithmetic  3.98 us (1%)
    psum x1, blocking collectives, per_device(): gain_total = lax.psum(gain_correction, 'expert')  127 us
    all_to_all x1, blocking collectives, per_device(): lax.all_to_all(rows_grad.reshape(peers, CAP, width), 'expert', split_axis...  56.9 us
    all_to_all x1, waiting for transfers between devices, per_device(): lax.all_to_all(send_x, 'expert', split_axis=0, concat_axis=0, tiled=True)  49.9 us
    all_to_all x1, waiting for transfers between devices, per_device(): lax.all_to_all(send_dy, 'expert', split_axis=0, concat_axis=0, tiled=True)  46.9 us
    all_to_all x1, blocking collectives, per_device(): lax.all_to_all(comb_part.reshape(peers, CAP), 'expert', split_axis=0, con...  15.2 us
    all_to_all x1, starting transfers between devices, per_device(): lax.all_to_all(send_w, 'expert', split_axis=0, concat_axis=0, tiled=True)  13.8 us
  transfers between devices with their start and end apart: 4, of which 3 were waited for; matrix products, arithmetic and copies ran while one was open for 3% of the time, Pallas kernels for 0%

commit v1 on v0

--- a/solution.py
+++ b/solution.py
@@ -140,7 +140,7 @@
         + reciprocal_norm * (scaled_gradient - normalized_rows * inner_product)
     ).astype(jnp.bfloat16)
     passed = from_behind(input_gradient, "section", -1)
-    gain_total = lax.psum(gain_correction, "expert")
+    gain_total = jnp.sum(lax.all_gather(gain_correction, "expert"), axis=0)
     return (passed[None], comb_out[None], gain_total[None])
 
 

time: 357 us -> 276 us (0.77)
  blocking collectives: 199 us -> 47.6 us
  waiting for transfers between devices: 104 us -> 158 us
  starting transfers between devices: 27.6 us -> 40 us
    psum x1 -> x0, blocking collectives: 127 us -> none  [per_device(): gain_total = lax.psum(gain_correction, 'expert')]
    all_to_all x2 -> x0, blocking collectives: 72 us -> none  [the longest x1 56.9 us: per_device(): lax.all_to_all(rows_grad.reshape(peers, CAP, width), 'expert', split_axis...]
    all_to_all x0 -> x2, waiting for transfers between devices: none -> 54.8 us  [the longest x1 50.8 us: per_device(): lax.all_to_all(rows_grad.reshape(peers, CAP, width), 'expert', split_axis...]
    all_gather x0 -> x1, blocking collectives: none -> 47.6 us  [per_device(): gain_total = jnp.sum(lax.all_gather(gain_correction, 'expert'), axis=0)]
    all_to_all x0 -> x2, starting transfers between devices: none -> 12.4 us  [the longest x1 6.48 us: per_device(): lax.all_to_all(rows_grad.reshape(peers, CAP, width), 'expert', split_axis...]
  transfers between devices with their start and end apart: 4 -> 6, of which waited for: 3 -> 5; matrix products, arithmetic and copies ran while one was open for 3% -> 5% of each run, Pallas kernels for 0% -> 0%
where the time goes in v1:
time: 276 us; the launch traced here: 275 us
  waiting for transfers between devices  158 us (57%)
  blocking collectives  47.6 us (17%)
  starting transfers between devices  40 us (14%)
  matrix products  15 us (5%)
  local copies, waits for them, and re-layouts  9.26 us (3%)
  other arithmetic  3.91 us (1%)
    all_to_all x1, waiting for transfers between devices, per_device(): lax.all_to_all(rows_grad.reshape(peers, CAP, width), 'expert', split_axis...  50.8 us
    all_to_all x1, waiting for transfers between devices, per_device(): lax.all_to_all(send_x, 'expert', split_axis=0, concat_axis=0, tiled=True)  49.9 us
    all_gather x1, blocking collectives, per_device(): gain_total = jnp.sum(lax.all_gather(gain_correction, 'expert'), axis=0)  47.6 us
    all_to_all x1, waiting for transfers between devices, per_device(): lax.all_to_all(send_dy, 'expert', split_axis=0, concat_axis=0, tiled=True)  46.9 us
    all_to_all x1, starting transfers between devices, per_device(): lax.all_to_all(send_w, 'expert', split_axis=0, concat_axis=0, tiled=True)  13.8 us
    all_to_all x1, waiting for transfers between devices, per_device(): lax.all_to_all(send_w, 'expert', split_axis=0, concat_axis=0, tiled=True)  6.72 us
    all_to_all x1, starting transfers between devices, per_device(): lax.all_to_all(rows_grad.reshape(peers, CAP, width), 'expert', split_axis...  6.48 us
    dot_general x3, matrix products, contract_cols(): lax.dot_general(left, right, (((1,), (1,)), ((), ())), preferred_element_...  6.3 us
  transfers between devices with their start and end apart: 6, of which 5 were waited for; matrix products, arithmetic and copies ran while one was open for 5% of the time, Pallas kernels for 0%

profile of v1, /device:TPU:56, one launch (start us, length us, event | category | flops | bytes accessed | tf_op | source)
XLA Modules:
  0.0 275.1 jit_solution(2855866110172505435)
XLA Ops:
  0.6 0.8 copy.33
  1.7 0.8 copy.37
  2.6 1.2 reduce-window.6
  4.4 0.6 copy.38
  5.0 13.8 %all-to-all-start = ((bf16[64,1,8]{2,1,0:T(2,128)(2,1)}), bf16[64,1,8]{2,1,0:T(2,128)(2,1)S(1)}, u32[]{:S(2)}, u32[]{:S(2)}) async-start(bf16[64,1,8]{2,1,0:T(2,128)(2,1)} %copy.38), calls=%async_computation | async-start | bytes 65536 | tf_op jit(solution)/shard_map/all_to_all | solution.py:106
  18.9 1.1 fusion.35
  20.2 1.3 fusion.5
  21.5 6.7 %all-to-all-done = bf16[64,1,8]{2,1,0:T(2,128)(2,1)S(1)} async-done(((bf16[64,1,8]{2,1,0:T(2,128)(2,1)}), bf16[64,1,8]{2,1,0:T(2,128)(2,1)S(1)}, u32[]{:S(2)}, u32[]{:S(2)}) %all-to-all-start) | async-done | bytes 1056 | tf_op jit(solution)/shard_map/all_to_all | solution.py:106
  28.2 1.6 broadcast_in_dim.23
  29.9 4.7 %all-to-all-start.2 = ((bf16[64,8,2048]{2,1,0:T(8,128)(2,1)}), bf16[64,8,2048]{2,1,0:T(8,128)(2,1)S(1)}, u32[]{:S(2)}, u32[]{:S(2)}) async-start(bf16[64,8,2048]{2,1,0:T(8,128)(2,1)} %bitcast.14), calls=%async_computation.2 | async-start | bytes 4194304 | tf_op jit(solution)/shard_map/all_to_all | solution.py:104
  34.6 1.3 fusion.4
  35.8 49.9 %all-to-all-done.2 = bf16[64,8,2048]{2,1,0:T(8,128)(2,1)S(1)} async-done(((bf16[64,8,2048]{2,1,0:T(8,128)(2,1)}), bf16[64,8,2048]{2,1,0:T(8,128)(2,1)S(1)}, u32[]{:S(2)}, u32[]{:S(2)}) %all-to-all-start.2) | async-done | bytes 2097184 | tf_op jit(solution)/shard_map/all_to_all | solution.py:104
  85.7 1.8 broadcast_in_dim.22
  87.7 5.9 %all-to-all-start.1 = ((bf16[64,8,2048]{2,1,0:T(8,128)(2,1)}), bf16[64,8,2048]{2,1,0:T(8,128)(2,1)S(1)}, u32[]{:S(2)}, u32[]{:S(2)}) async-start(bf16[64,8,2048]{2,1,0:T(8,128)(2,1)} %bitcast.8), calls=%async_computation.1 | async-start | bytes 4194304 | tf_op jit(solution)/shard_map/all_to_all | solution.py:105
  93.7 2.6 fusion.9
  96.3 1.6 fusion.11
  97.9 46.9 %all-to-all-done.1 = bf16[64,8,2048]{2,1,0:T(8,128)(2,1)S(1)} async-done(((bf16[64,8,2048]{2,1,0:T(8,128)(2,1)}), bf16[64,8,2048]{2,1,0:T(8,128)(2,1)S(1)}, u32[]{:S(2)}, u32[]{:S(2)}) %all-to-all-start.1) | async-done | bytes 2097184 | tf_op jit(solution)/shard_map/all_to_all | solution.py:105
  144.8 2.1 fusion.2
  146.9 0.7 convert_element_type.145
  147.6 5.9 %all-to-all-start.4 = ((bf16[64,1,8]{2,1,0:T(2,128)(2,1)}), bf16[64,1,8]{2,1,0:T(2,128)(2,1)S(1)}, u32[]{:S(2)}, u32[]{:S(2)}) async-start(bf16[64,1,8]{2,1,0:T(2,128)(2,1)} %convert_element_type.145), calls=%async_computation.4 | async-start | bytes 65536 | tf_op jit(solution)/shard_map/all_to_all | solution.py:122
  153.5 2.1 fusion.7
  155.7 0.8 fusion.17
  156.8 2.1 fusion.3
  158.9 4.0 %all-to-all-done.4 = bf16[64,1,8]{2,1,0:T(2,128)(2,1)S(1)} async-done(((bf16[64,1,8]{2,1,0:T(2,128)(2,1)}), bf16[64,1,8]{2,1,0:T(2,128)(2,1)S(1)}, u32[]{:S(2)}, u32[]{:S(2)}) %all-to-all-start.4) | async-done | bytes 1056 | tf_op jit(solution)/shard_map/all_to_all | solution.py:122
  163.0 6.5 %all-to-all-start.3 = ((bf16[64,8,2048]{2,1,0:T(8,128)(2,1)}), bf16[64,8,2048]{2,1,0:T(8,128)(2,1)S(1)}, u32[]{:S(2)}, u32[]{:S(2)}) async-start(bf16[64,8,2048]{2,1,0:T(8,128)(2,1)} %fusion.3), calls=%async_computation.3 | async-start | bytes 4194304 | tf_op jit(solution)/shard_map/all_to_all | solution.py:119
  169.6 50.8 %all-to-all-done.3 = bf16[64,8,2048]{2,1,0:T(8,128)(2,1)S(1)} async-done(((bf16[64,8,2048]{2,1,0:T(8,128)(2,1)}), bf16[64,8,2048]{2,1,0:T(8,128)(2,1)S(1)}, u32[]{:S(2)}, u32[]{:S(2)}) %all-to-all-start.3) | async-done | bytes 2097184 | tf_op jit(solution)/shard_map/all_to_all | solution.py:119
  220.8 0.7 fusion.34
  221.8 3.3 %collective-permute-start = (bf16[64,2048]{1,0:T(8,128)(2,1)S(1)}, bf16[64,2048]{1,0:T(8,128)(2,1)S(1)}, u32[]{:S(2)}, u32[]{:S(2)}) collective-permute-start(bf16[64,2048]{1,0:T(8,128)(2,1)S(1)} %fusion.33), channel_id=1, source_target_pairs={{64,0},{128,64},{192,128},{256,192},{320,256},{384,320},{448,384},... | collective-permute-start | bytes 786440 | tf_op jit(solution)/shard_map/ppermute | solution.py:14
  225.4 0.7 copy.40
  226.0 47.6 %all-gather = f32[131072]{0:T(1024)S(1)} all-gather(f32[2048]{0:T(1024)S(1)} %get-tuple-element.15), channel_id=2, replica_groups=mesh['section'=8,'expert'=64] {'expert'}, dimensions={0}, use_global_device_ids=true | all-gather | bytes 532480 | tf_op jit(solution)/shard_map/all_gather | solution.py:143
  273.8 0.6 reduce_sum.95
  274.4 0.7 copy.44
  (46 shorter events, 2.8 us)
Async XLA Ops:
  0.6 93.0 %copy-start = (bf16[1,192,2048]{2,1,0:T(8,128)(2,1)S(1)}, bf16[1,192,2048]{2,1,0:T(8,128)(2,1)}, u32[]{:S(2)}) copy-start(bf16[1,192,2048]{2,1,0:T(8,128)(2,1)} %param.13) | copy-start | bytes 2359300
  5.0 23.2 %all-to-all-start = ((bf16[64,1,8]{2,1,0:T(2,128)(2,1)}), bf16[64,1,8]{2,1,0:T(2,128)(2,1)S(1)}, u32[]{:S(2)}, u32[]{:S(2)}) async-start(bf16[64,1,8]{2,1,0:T(2,128)(2,1)} %copy.38), calls=%async_computation | async-start | bytes 65536 | tf_op jit(solution)/shard_map/all_to_all | solution.py:106
  29.9 55.9 %all-to-all-start.2 = ((bf16[64,8,2048]{2,1,0:T(8,128)(2,1)}), bf16[64,8,2048]{2,1,0:T(8,128)(2,1)S(1)}, u32[]{:S(2)}, u32[]{:S(2)}) async-start(bf16[64,8,2048]{2,1,0:T(8,128)(2,1)} %bitcast.14), calls=%async_computation.2 | async-start | bytes 4194304 | tf_op jit(solution)/shard_map/all_to_all | solution.py:104
  85.7 2.0 copy-start.2
  87.7 57.1 %all-to-all-start.1 = ((bf16[64,8,2048]{2,1,0:T(8,128)(2,1)}), bf16[64,8,2048]{2,1,0:T(8,128)(2,1)S(1)}, u32[]{:S(2)}, u32[]{:S(2)}) async-start(bf16[64,8,2048]{2,1,0:T(8,128)(2,1)} %bitcast.8), calls=%async_computation.1 | async-start | bytes 4194304 | tf_op jit(solution)/shard_map/all_to_all | solution.py:105
  93.7 2.6 copy-start.3
  93.7 2.6 copy-start.5
  147.6 15.3 %all-to-all-start.4 = ((bf16[64,1,8]{2,1,0:T(2,128)(2,1)}), bf16[64,1,8]{2,1,0:T(2,128)(2,1)S(1)}, u32[]{:S(2)}, u32[]{:S(2)}) async-start(bf16[64,1,8]{2,1,0:T(2,128)(2,1)} %convert_element_type.145), calls=%async_computation.4 | async-start | bytes 65536 | tf_op jit(solution)/shard_map/all_to_all | solution.py:122
  153.5 2.1 copy-start.7
  155.7 1.1 copy-start.6
  163.0 57.5 %all-to-all-start.3 = ((bf16[64,8,2048]{2,1,0:T(8,128)(2,1)}), bf16[64,8,2048]{2,1,0:T(8,128)(2,1)S(1)}, u32[]{:S(2)}, u32[]{:S(2)}) async-start(bf16[64,8,2048]{2,1,0:T(8,128)(2,1)} %fusion.3), calls=%async_computation.3 | async-start | bytes 4194304 | tf_op jit(solution)/shard_map/all_to_all | solution.py:119
  169.4 51.4 %copy-start.1 = (bf16[1,64,2048]{2,1,0:T(8,128)(2,1)S(1)}, bf16[1,64,2048]{2,1,0:T(8,128)(2,1)}, u32[]{:S(2)}) copy-start(bf16[1,64,2048]{2,1,0:T(8,128)(2,1)} %param.8) | copy-start | bytes 786436
  169.4 51.4 %copy-start.8 = (f32[1,2048]{1,0:T(1,128)S(1)}, f32[1,2048]{1,0:T(1,128)}, u32[]{:S(2)}) copy-start(f32[1,2048]{1,0:T(1,128)} %param.10) | copy-start | bytes 24580
  169.6 51.9 %copy-start.4 = (bf16[1,64,2048]{2,1,0:T(8,128)(2,1)S(1)}, bf16[1,64,2048]{2,1,0:T(8,128)(2,1)}, u32[]{:S(2)}) copy-start(bf16[1,64,2048]{2,1,0:T(8,128)(2,1)} %param.9) | copy-start | bytes 786436
  221.8 52.6 %collective-permute-start = (bf16[64,2048]{1,0:T(8,128)(2,1)S(1)}, bf16[64,2048]{1,0:T(8,128)(2,1)S(1)}, u32[]{:S(2)}, u32[]{:S(2)}) collective-permute-start(bf16[64,2048]{1,0:T(8,128)(2,1)S(1)} %fusion.33), channel_id=1, source_target_pairs={{64,0},{128,64},{192,128},{256,192},{320,256},{384,320},{448,384},... | collective-permute-start | bytes 786440 | tf_op jit(solution)/shard_map/ppermute | solution.py:14
